TPU v7x, 512 devices: a whole 4x8x8 slice. The times are simulated.
512 devices in a mesh: tm: 32 (over z_hi, y), chan: 16 (over z_lo, x, core).
Axes of the slice: x: 4, y: 8, z: 8 (z_hi: 4, z_lo: 2; z = z_hi * 2 + z_lo), core: 2. Of those that a mesh axis runs over, the one named last changes fastest.
Arguments:
- raw: bfloat16 [8192, 12288], P('tm', 'chan'), may hold values from -6 to 6
- taper: float32 [1024], replicated, may hold values from 0.1 to 1
- depth_owner: int32 [12288, 2], P('chan'), may hold values from 0 to 15, all different within a row; in each aligned block of 24 rows (0 to 23, 24 to 47, ...) at most 6 rows name the same one
- depth_slot: int32 [12288, 2], P('chan'), may hold values from 0 to 255
- intersection: int32 [12288, 2], P('chan'), may hold values from 1 to 100
Outputs:
- stacked: float32 [2, 4096, 1024], P(None, 'chan', 'tm')
Inputs may be any that keep to these rules, and one draw needn't show every extreme that they name: `depth_owner`: the 2 owner groups of one channel differ. In each aligned block of 24 channels no owner group is named by more than 6 channels, and some owner group is named by exactly 6 channels.
All inputs are finite; a program needn't handle non-finite values.
Results may differ from a plain program's by a relative error of at most 0.0003.
Values may be sent and summed in bfloat16 or wider, within the bound.
A program may use at most 64 MiB of HBM per device.

v0:
```python
import math

import jax
import jax.numpy as jnp
from jax import lax
from jax.sharding import PartitionSpec as P

N1 = 128
N2 = 64
NT = 8192
KLO = 128
NB = 1024
K = 2
B_OWN = 256


HIGHEST = lax.Precision.HIGHEST


def spectrum_rows(samples_in, band_scale):
    count_items = samples_in.shape[2]
    samples = samples_in.reshape(N1, N2 * count_items).astype(jnp.float32)
    k_one = jnp.arange(N1, dtype=jnp.int32)
    angle_one = (k_one[:, None] * k_one[None, :] % N1).astype(jnp.float32) * (2.0 * math.pi / N1)
    real_one = jnp.dot(jnp.cos(angle_one), samples, precision=HIGHEST).reshape(N1, N2, count_items)
    imag_one = -jnp.dot(jnp.sin(angle_one), samples, precision=HIGHEST).reshape(N1, N2, count_items)
    t_two = jnp.arange(N2, dtype=jnp.int32)
    angle_mid = (k_one[:, None] * t_two[None, :] % (N1 * N2)).astype(jnp.float32) * (
        2.0 * math.pi / (N1 * N2)
    )
    cos_mid = jnp.cos(angle_mid)[:, :, None]
    sin_mid = jnp.sin(angle_mid)[:, :, None]
    real_mid = real_one * cos_mid + imag_one * sin_mid
    imag_mid = imag_one * cos_mid - real_one * sin_mid
    k_band = KLO // N1 + jnp.arange(NB // N1, dtype=jnp.int32)
    angle_two = (t_two[:, None] * k_band[None, :] % N2).astype(jnp.float32) * (2.0 * math.pi / N2)
    cos_two = jnp.cos(angle_two)
    sin_two = jnp.sin(angle_two)
    real_out = jnp.einsum("atn,tb->nba", real_mid, cos_two, precision=HIGHEST) + jnp.einsum(
        "atn,tb->nba", imag_mid, sin_two, precision=HIGHEST
    )
    imag_out = jnp.einsum("atn,tb->nba", imag_mid, cos_two, precision=HIGHEST) - jnp.einsum(
        "atn,tb->nba", real_mid, sin_two, precision=HIGHEST
    )
    real_out = real_out.reshape(count_items, NB) * band_scale[None, :]
    imag_out = imag_out.reshape(count_items, NB) * band_scale[None, :]
    return jnp.stack([real_out, imag_out], 1)


def pack_entries(entry_rows, owner_list, slot_list, weights, blocks, block_rows, capacity, groups):
    channels = owner_list.shape[0]
    cols = entry_rows.shape[1]
    flat_owner = owner_list.reshape(-1)
    onehot = (
        flat_owner.reshape(blocks, block_rows * K)[:, :, None]
        == jnp.arange(groups, dtype=jnp.int32)[None, None, :]
    ).astype(jnp.int32)
    before_rank = jnp.sum((jnp.cumsum(onehot, axis=1) - onehot) * onehot, axis=2).reshape(-1)
    block_id = jnp.arange(channels * K, dtype=jnp.int32) // (block_rows * K)
    slot_index = flat_owner * (blocks * capacity) + block_id * capacity + before_rank
    weighted = (entry_rows[:, None, :] * weights[:, :, None]).reshape(channels * K, cols)
    total_slots = groups * blocks * capacity
    outgoing = jnp.zeros((total_slots, cols), jnp.float32).at[slot_index].set(weighted)
    tag_rows = jnp.stack([weights.reshape(-1), slot_list.reshape(-1).astype(jnp.float32)], 1)
    tags = jnp.zeros((total_slots, 2), jnp.float32).at[slot_index].set(tag_rows)
    return (
        outgoing.reshape(groups, blocks * capacity, cols),
        tags.reshape(groups, blocks * capacity, 2),
    )


def stack_bins(arrived, tags):
    cols = arrived.shape[2]
    arrived_rows = arrived.reshape(-1, cols)
    bin_index = tags[:, :, 1].reshape(-1).astype(jnp.int32)
    arrived_weight = tags[:, :, 0].reshape(-1)
    stack_sum = jax.ops.segment_sum(arrived_rows, bin_index, num_segments=B_OWN)
    weight_sum = jax.ops.segment_sum(arrived_weight, bin_index, num_segments=B_OWN)
    return (stack_sum, weight_sum)


def local(raw, taper, depth_owner, depth_slot, intersection):
    tm_count = lax.axis_size("tm")
    chan_count = lax.axis_size("chan")
    rows_here = raw.shape[1] // tm_count
    band_scale = taper * (1.0 / math.sqrt(NT))
    grouped = raw.reshape(raw.shape[0], tm_count, rows_here)
    spectra = spectrum_rows(
        lax.all_to_all(grouped, "tm", split_axis=1, concat_axis=0, tiled=True),
        band_scale=band_scale,
    )
    capacity = max(2, min(rows_here, 2 * rows_here * K // chan_count))
    weights_all = intersection.astype(jnp.float32)
    first_row = lax.axis_index("tm") * rows_here
    own_owner = lax.dynamic_slice_in_dim(depth_owner, first_row, rows_here, 0)
    own_slot = lax.dynamic_slice_in_dim(depth_slot, first_row, rows_here, 0)
    own_weight = lax.dynamic_slice_in_dim(weights_all, first_row, rows_here, 0)
    outgoing, tags = pack_entries(
        spectra.reshape(rows_here, 2 * NB),
        own_owner,
        own_slot,
        own_weight,
        1,
        rows_here,
        capacity,
        chan_count,
    )
    arrived, tags_in = (
        lax.all_to_all(outgoing, "chan", split_axis=0, concat_axis=0, tiled=True),
        lax.all_to_all(tags, "chan", split_axis=0, concat_axis=0, tiled=True),
    )
    stack_sum, weight_sum = stack_bins(arrived, tags_in)
    partial_stack = stack_sum.reshape(B_OWN, 2, NB).transpose(1, 0, 2)
    folded = lax.psum_scatter(partial_stack, "tm", scatter_dimension=2, tiled=True)
    weight_total = lax.psum(weight_sum, "tm")
    return folded / jnp.maximum(weight_total, 1.0)[None, :, None]


def solution(mesh):
    return jax.shard_map(
        local,
        mesh=mesh,
        in_specs=(P("tm", "chan"), P(), P("chan", None), P("chan", None), P("chan", None)),
        out_specs=P(None, "chan", "tm"),
        check_vma=False,
    )
```

profile of v0, /device:TPU:1, one launch (start us, length us, event | category | flops | bytes accessed | tf_op | source)
XLA Modules:
  0.0 309.5 jit_solution(16059040889019355632)
XLA Ops:
  6.5 1.9 copy.49
  8.5 16.5 %all-to-all-start.1 = ((bf16[256,32,24]{0,2,1:T(8,128)(2,1)}), bf16[256,32,24]{0,2,1:T(8,128)(2,1)S(1)}, u32[]{:S(2)}, u32[]{:S(2)}) async-start(bf16[256,32,24]{0,2,1:T(8,128)(2,1)} %bitcast.4), calls=%async_computation.1 | async-start | bytes 786432 | tf_op jit(solution)/shard_map/all_to_all | solution.py:89
  25.0 0.8 dynamic-slice_convert_fusion
  25.8 0.1 copy.44
  25.8 0.1 mul.255
  25.9 0.1 stack_reshape.3
  26.0 0.1 constant_dynamic-slice_fusion
  26.1 0.1 copy.42
  26.2 0.1 eq.33
  26.3 0.1 reshape.310
  26.4 0.1 copy.45
  26.5 0.1 convert_element_type.78
  26.6 0.1 copy.46
  26.7 0.1 fusion.31
  26.8 0.1 reduce_window_sum.11
  26.9 0.2 select_reduce_fusion
  27.1 0.7 scatter_custom_fusion
  27.8 0.1 copy.47
  27.8 0.1 reshape.311
  27.9 0.6 copy.48
  28.6 0.1 fusion.34
  28.7 0.7 broadcast_multiply_fusion.2
  29.4 10.2 %all-to-all-done.1 = bf16[256,32,24]{0,2,1:T(8,128)(2,1)S(1)} async-done(((bf16[256,32,24]{0,2,1:T(8,128)(2,1)}), bf16[256,32,24]{0,2,1:T(8,128)(2,1)S(1)}, u32[]{:S(2)}, u32[]{:S(2)}) %all-to-all-start.1) | async-done | bytes 393248 | tf_op jit(solution)/shard_map/all_to_all | solution.py:89
  39.7 8.4 %all-to-all-start = ((f32[16,6,2]{1,2,0:T(2,128)}), f32[16,6,2]{1,2,0:T(2,128)S(1)}, u32[]{:S(2)}, u32[]{:S(2)}) async-start(f32[16,6,2]{1,2,0:T(2,128)} %copy.48), calls=%async_computation | async-start | bytes 32768 | tf_op jit(solution)/shard_map/all_to_all | solution.py:110
  48.1 1.0 copy.50
  49.1 3.7 %reshape.313 = bf16[128,1536]{1,0:T(8,128)(2,1)S(1)} reshape(bf16[32,256,1,24]{3,1,0,2:T(8,128)(2,1)S(1)} %copy.50) | data formatting | bytes 786432 | tf_op jit(solution)/shard_map/reshape | solution.py:22
  52.8 0.2 copy.51
  53.0 0.7 convolution_negate_fusion
  53.8 0.7 fusion.8
  54.5 0.6 fusion.11
  55.1 0.6 fusion.10
  55.7 0.6 fusion
  56.4 0.6 fusion.1
  57.1 0.2 mul.253
  57.3 0.3 mul.254
  57.6 1.1 scatter_custom_fusion.1
  58.7 1.1 reshape.316
  59.8 5.7 %all-to-all-start.2 = ((f32[16,6,2048]{2,1,0:T(8,128)}), f32[16,6,2048]{2,1,0:T(8,128)S(1)}, u32[]{:S(2)}, u32[]{:S(2)}) async-start(f32[16,6,2048]{2,1,0:T(8,128)} %reshape.316), calls=%async_computation.2 | async-start | bytes 2097152 | tf_op jit(solution)/shard_map/all_to_all | solution.py:109
  65.6 0.1 reshape.337
  65.7 15.7 %all-to-all-done.2 = f32[16,6,2048]{2,1,0:T(8,128)S(1)} async-done(((f32[16,6,2048]{2,1,0:T(8,128)}), f32[16,6,2048]{2,1,0:T(8,128)S(1)}, u32[]{:S(2)}, u32[]{:S(2)}) %all-to-all-start.2) | async-done | bytes 786464 | tf_op jit(solution)/shard_map/all_to_all | solution.py:109
  81.4 0.1 reshape.339
  81.5 2.3 scatter_custom_fusion.2
  83.8 1.9 copy.57
  85.7 0.1 reshape.347
  85.8 1.2 scatter_custom_fusion.3
  87.0 65.2 %psum.7 = f32[256]{0:T(256)S(1)} all-reduce(f32[256]{0:T(256)S(1)} %scatter_custom_fusion.3), channel_id=1, replica_groups=mesh['tm'=32,'chan'=16] {'tm'}, use_global_device_ids=true, to_apply=%region_7.8 | all-reduce | flops 256 | bytes 2048 | tf_op jit(solution)/shard_map/psum | solution.py:115
  152.2 149.0 %reduce-scatter.2.cloned.1.call-done = f32[2,256,32]{1,2,0:T(8,128)} async-done(((f32[2,256,1024]{1,2,0:T(8,128)}), f32[2,256,32]{1,2,0:T(8,128)}) %reduce-scatter.2.cloned.1.call-update) | async-done | bytes 65552 | tf_op jit(solution)/shard_map/reduce_scatter | solution.py:114
  301.2 1.5 broadcast_divide_fusion
  (16 shorter events, 0.2 us)
Async XLA Ops:
  6.5 19.5 %copy-start = (s32[768,2]{0,1:T(2,128)S(1)}, s32[768,2]{0,1:T(2,128)}, u32[]{:S(2)}) copy-start(s32[768,2]{0,1:T(2,128)} %param.7) | copy-start | bytes 18436
  8.5 31.2 %all-to-all-start.1 = ((bf16[256,32,24]{0,2,1:T(8,128)(2,1)}), bf16[256,32,24]{0,2,1:T(8,128)(2,1)S(1)}, u32[]{:S(2)}, u32[]{:S(2)}) async-start(bf16[256,32,24]{0,2,1:T(8,128)(2,1)} %bitcast.4), calls=%async_computation.1 | async-start | bytes 786432 | tf_op jit(solution)/shard_map/all_to_all | solution.py:89
  39.7 20.2 %all-to-all-start = ((f32[16,6,2]{1,2,0:T(2,128)}), f32[16,6,2]{1,2,0:T(2,128)S(1)}, u32[]{:S(2)}, u32[]{:S(2)}) async-start(f32[16,6,2]{1,2,0:T(2,128)} %copy.48), calls=%async_computation | async-start | bytes 32768 | tf_op jit(solution)/shard_map/all_to_all | solution.py:110
  59.8 21.6 %all-to-all-start.2 = ((f32[16,6,2048]{2,1,0:T(8,128)}), f32[16,6,2048]{2,1,0:T(8,128)S(1)}, u32[]{:S(2)}, u32[]{:S(2)}) async-start(f32[16,6,2048]{2,1,0:T(8,128)} %reshape.316), calls=%async_computation.2 | async-start | bytes 2097152 | tf_op jit(solution)/shard_map/all_to_all | solution.py:109
  65.6 235.6 %reduce-scatter.2.cloned.1.call-start = ((), (), s32[]{:S(2)}) async-start(), calls=%async_computation.4 | async-start | bytes 2162688 | tf_op jit(solution)/shard_map/reduce_scatter | solution.py:114
Sparse Core Ops, SparseCore 0:
  85.8 215.3 reduce-scatter.1
where the time goes:
time: 314 us; the launch traced here: 310 us
  waiting for transfers between devices  175 us (56%)
  blocking collectives  65.2 us (21%)
  starting transfers between devices  30.7 us (10%)
  between operations  13.6 us (4%)
  local copies, waits for them, and re-layouts  13.1 us (4%)
  other arithmetic  8.11 us (3%)
  matrix products  3.95 us (1%)
    reduce_scatter x1, waiting for transfers between devices, local(): lax.psum_scatter(partial_stack, 'tm', scatter_dimension=2, tiled=True)  149 us
    psum x1, blocking collectives, local(): weight_total = lax.psum(weight_sum, 'tm')  65.2 us
    all_to_all x1, starting transfers between devices, local(): lax.all_to_all(grouped, 'tm', split_axis=1, concat_axis=0, tiled=True)  16.5 us
    all_to_all x1, waiting for transfers between devices, local(): lax.all_to_all(outgoing, 'chan', split_axis=0, concat_axis=0, tiled=True)  15.7 us
    all_to_all x1, waiting for transfers between devices, local(): lax.all_to_all(grouped, 'tm', split_axis=1, concat_axis=0, tiled=True)  10.2 us
    all_to_all x1, starting transfers between devices, local(): lax.all_to_all(tags, 'chan', split_axis=0, concat_axis=0, tiled=True)  8.43 us
  transfers between devices with their start and end apart: 4, of which 3 were waited for; matrix products, arithmetic and copies ran while one was open for 6% of the time, Pallas kernels for 0%

commit v1 on v0

v1 whole, which is shorter than its diff:
```python
import math

import jax
import jax.numpy as jnp
import numpy as np
from jax import lax
from jax.experimental import pallas as pl
from jax.experimental.pallas import tpu as pltpu
from jax.sharding import PartitionSpec as P

NT = 8192
KLO = 128
NB = 1024
B_OWN = 256
N_TM = 32
N_CHAN = 16
CH = 768
TB = 256
TC = 64
NX = 4
BF = jnp.bfloat16
F32 = jnp.float32
MESH = pl.DeviceIdType.MESH


def split_np(a):
    hi = a.astype(jnp.bfloat16)
    lo = (a - hi.astype(np.float64)).astype(jnp.bfloat16)
    return hi, lo


def tables():
    p = np.arange(32)
    s = np.arange(TB)
    ang = 2.0 * np.pi * (np.outer(p, p) % 32) / 32
    first = np.concatenate([np.cos(ang), -np.sin(ang)], 0)
    hi, lo = split_np(first)
    first = np.concatenate([hi, hi, lo], 1)
    mid = 2.0 * np.pi * np.outer(p, s) / NT
    twiddle = np.stack([np.cos(mid), np.sin(mid)]).astype(np.float32)
    q = KLO // 32 + np.arange(NB // 32)
    ang = 2.0 * np.pi * (np.outer(q, s) % TB) / TB
    c, z = np.cos(ang), np.sin(ang)
    second = np.concatenate([np.concatenate([c, z], 1), np.concatenate([-z, c], 1)], 0)
    hi, lo = split_np(second)
    second = np.concatenate([hi, hi, lo], 1)
    return first, twiddle, second


def split(a):
    hi = a.astype(BF)
    lo = (a - hi.astype(F32)).astype(BF)
    return hi, lo


def kernel(
    raw, code, first, twiddle, second, taper, out,
    blocks, codes, acc, packed, parts, rows, samples, mid, outgo, arrived,
    send_raw, recv_raw, send_code, recv_code, fsend_raw, frecv_raw, fsend_code, frecv_code,
    send_x, recv_x, send_t, recv_t, send_f, recv_f, own_sem,
):
    me = lax.axis_index("tm")
    g = lax.axis_index("chan")
    core, x, zl = lax.rem(g, 2), lax.rem(g // 2, NX), g // 8

    def place(dz, dx):
        return (lax.rem(zl + dz, 2) * NX + lax.rem(x + dx, NX)) * 2 + core

    steps = [(0, 0), (1, 0), (0, 1), (1, 1), (0, 3), (1, 3), (0, 2), (1, 2)]
    partner = g + 1 - 2 * core

    barrier = pltpu.get_barrier_semaphore()
    for dz, dx in steps[1:]:
        pl.semaphore_signal(barrier, inc=1, device_id=(me, place(dz, dx)), device_id_type=MESH)
    pl.semaphore_signal(barrier, inc=1, device_id=(me, partner), device_id_type=MESH)

    def greet(d, _):
        pl.semaphore_signal(barrier, inc=1, device_id=(lax.rem(me + d, N_TM), g), device_id_type=MESH)
        return 0

    lax.fori_loop(1, N_TM, greet, 0)
    own_raw = pltpu.make_async_copy(raw.at[pl.ds(pl.multiple_of(x * TC, TC), TC), :], blocks.at[g], own_sem.at[0])
    own_code = pltpu.make_async_copy(code, codes.at[g], own_sem.at[1])
    own_raw.start()
    own_code.start()
    pl.semaphore_wait(barrier, 8 + N_TM - 1)

    def raw_copy(k, dz, dx):
        chunk = pl.ds(pl.multiple_of(lax.rem(x + dx, NX) * TC, TC), TC)
        return pltpu.make_async_remote_copy(
            src_ref=raw.at[chunk, :], dst_ref=blocks.at[g],
            send_sem=send_raw.at[k], recv_sem=recv_raw.at[k],
            device_id=(me, place(dz, dx)), device_id_type=MESH,
        )

    def code_copy(k, dz, dx):
        return pltpu.make_async_remote_copy(
            src_ref=code, dst_ref=codes.at[g],
            send_sem=send_code.at[k], recv_sem=recv_code.at[k],
            device_id=(me, place(dz, dx)), device_id_type=MESH,
        )

    for k, (dz, dx) in enumerate(steps):
        if k:
            code_copy(k, dz, dx).start()
            raw_copy(k, dz, dx).start()

    def forward(k, src):
        return (
            pltpu.make_async_remote_copy(
                src_ref=codes.at[src], dst_ref=codes.at[src],
                send_sem=fsend_code.at[k], recv_sem=frecv_code.at[k],
                device_id=(me, partner), device_id_type=MESH,
            ),
            pltpu.make_async_remote_copy(
                src_ref=blocks.at[src], dst_ref=blocks.at[src],
                send_sem=fsend_raw.at[k], recv_sem=frecv_raw.at[k],
                device_id=(me, partner), device_id_type=MESH,
            ),
        )

    slot_of_row = lax.broadcasted_iota(jnp.int32, (B_OWN, 128), 0).astype(F32).astype(BF)
    ones = jnp.ones((TC, 256), BF)
    acc[...] = jnp.zeros_like(acc)

    def weights_of(src, owner, m):
        c0 = codes[src, pl.ds(m, 1), :]
        c1 = codes[src, pl.ds(6 + m, 1), :]
        c = jnp.where((c0 >> 15) == owner, c0, jnp.where((c1 >> 15) == owner, c1, -1))
        slot = jnp.where(c < 0, -1, (c >> 7) & 255).astype(F32)
        weight = (c & 127).astype(F32)
        slot = jnp.broadcast_to(slot, (16, 128)).astype(BF)
        weight = jnp.broadcast_to(weight, (16, 128)).astype(BF)
        slot = jnp.concatenate([slot] * (B_OWN // 16), 0)
        weight = jnp.concatenate([weight] * (B_OWN // 16), 0)
        return jnp.where(slot_of_row == slot, weight, BF(0))

    def process(src):
        data = [
            jnp.concatenate([blocks[src, :, pl.ds(256 * mm, 256)], ones], 0)
            for mm in range(CH // 256)
        ]
        for xo in range(NX):
            owner = (zl * NX + xo) * 2 + core
            total = None
            for mm in range(CH // 256):
                sel = jnp.concatenate(
                    [weights_of(src, owner, 2 * mm), weights_of(src, owner, 2 * mm + 1)], 1
                )
                part = lax.dot_general(
                    sel, data[mm], (((1,), (1,)), ((), ())), preferred_element_type=F32
                )
                total = part if total is None else total + part
            acc[pl.ds(B_OWN * xo, B_OWN), :] += total

    own_raw.wait()
    own_code.wait()
    for copy in forward(0, g):
        copy.start()
    process(g)
    for copy in forward(0, g + 1 - 2 * core):
        copy.wait_recv()
    process(partner)

    def step(k, _):
        dz = lax.rem(k, 2)
        dx = k // 2
        dx = dx + jnp.where(dx == 2, 1, jnp.where(dx == 3, -1, 0))
        src = (lax.rem(zl + 2 - dz, 2) * NX + lax.rem(x + NX - dx, NX)) * 2 + core
        code_copy(k, dz, dx).wait_recv()
        raw_copy(k, dz, dx).wait_recv()
        for copy in forward(k, src):
            copy.start()
        process(src)
        other = src + 1 - 2 * core
        for copy in forward(k, other):
            copy.wait_recv()
        process(other)
        return 0

    lax.fori_loop(1, 8, step, 0)

    left = lax.broadcasted_iota(jnp.int32, (128, 128), 1) < TC

    def x_copy(dx):
        xo = lax.rem(x + dx, NX)
        return pltpu.make_async_remote_copy(
            src_ref=packed.at[xo], dst_ref=parts.at[x],
            send_sem=send_x.at[dx], recv_sem=recv_x.at[dx],
            device_id=(me, place(0, dx)), device_id_type=MESH,
        )

    def means(r):
        a = acc[pl.ds(r, 128), :]
        return a / jnp.maximum(pltpu.roll(a, TC, 1), 1.0)

    for xo in range(NX):
        low = means(B_OWN * xo)
        high = means(B_OWN * xo + 128)
        packed[xo] = jnp.where(left, low, pltpu.roll(high, TC, 1))
    for dx in (2, 1, 3):
        x_copy(dx).start()
    parts[x] = packed[x]
    for dx in (1, 3, 2):
        x_copy(dx).wait_recv()
    for h in range(2):
        a, b = parts[2 * h], parts[2 * h + 1]
        low = jnp.where(left, a, pltpu.roll(b, TC, 1)).reshape(16, 8, 128)
        high = jnp.where(left, pltpu.roll(a, TC, 1), b).reshape(16, 8, 128)
        rows[pl.ds(0, 16), pl.ds(8 * h, 8), :] = low
        rows[pl.ds(16, 16), pl.ds(8 * h, 8), :] = high

    def eight(i):
        return pl.ds(pl.multiple_of(i * 8, 8), 8)

    def sixteen(i):
        return pl.ds(pl.multiple_of(i * 16, 16), 16)

    def send_rows(d, _):
        to = lax.rem(me + d, N_TM)
        pltpu.make_async_remote_copy(
            src_ref=rows.at[to], dst_ref=samples.at[sixteen(me), :],
            send_sem=send_t, recv_sem=recv_t, device_id=(to, g), device_id_type=MESH,
        ).start()
        return 0

    lax.fori_loop(1, N_TM, send_rows, 0)
    samples[sixteen(me), :] = rows[me]
    all_t = pltpu.make_async_remote_copy(
        src_ref=samples.at[pl.ds(0, 16 * (N_TM - 1)), :],
        dst_ref=samples.at[pl.ds(0, 16 * (N_TM - 1)), :],
        send_sem=send_t, recv_sem=recv_t, device_id=(me, partner), device_id_type=MESH,
    )
    all_t.wait_recv()

    cos, sin = twiddle[0], twiddle[1]
    for b in range(8):
        hi, lo = split(
            jnp.concatenate([samples[pl.ds(b, N_TM, 16), :], samples[pl.ds(8 + b, N_TM, 16), :]], 1)
        )
        y = jnp.dot(first[...], jnp.concatenate([hi, lo, hi], 0), preferred_element_type=F32)
        re, im = y[:32], y[32:]
        z = jnp.concatenate([re * cos + im * sin, im * cos - re * sin], 1)
        hi, lo = split(z)
        mid[pl.ds(32 * b, 32), pl.ds(0, 512)] = hi
        mid[pl.ds(32 * b, 32), pl.ds(512, 512)] = lo
        mid[pl.ds(32 * b, 32), pl.ds(1024, 512)] = hi
    spec = lax.dot_general(
        second[...], mid[...], (((1,), (1,)), ((), ())), preferred_element_type=F32
    )
    outgo[...] = jnp.zeros_like(outgo)
    for r in range(2):
        band = spec[32 * r : 32 * r + 32] * taper[...]
        for h in range(2):
            outgo[pl.ds(2 * r + h, 32, 8), :] = band[:, 128 * h : 128 * h + 128]

    def send_band(d, _):
        to = lax.rem(me + d, N_TM)
        pltpu.make_async_remote_copy(
            src_ref=outgo.at[eight(to), :], dst_ref=arrived.at[eight(me), :],
            send_sem=send_f, recv_sem=recv_f, device_id=(to, g), device_id_type=MESH,
        ).start()
        return 0

    lax.fori_loop(1, N_TM, send_band, 0)
    arrived[eight(me), :] = outgo[eight(me), :]
    all_f = pltpu.make_async_remote_copy(
        src_ref=outgo.at[pl.ds(0, 8 * (N_TM - 1)), :], dst_ref=arrived.at[pl.ds(0, 8 * (N_TM - 1)), :],
        send_sem=send_f, recv_sem=recv_f, device_id=(me, partner), device_id_type=MESH,
    )
    all_f.wait_recv()
    out[...] = arrived[...]

    for k, (dz, dx) in enumerate(steps):
        if k:
            code_copy(k, dz, dx).wait_send()
            raw_copy(k, dz, dx).wait_send()
        for copy in forward(k, g):
            copy.wait_send()
    for dx in (1, 3, 2):
        x_copy(dx).wait_send()
    all_t.wait_send()
    all_f.wait_send()


def local(raw, taper, depth_owner, depth_slot, intersection):
    first, twiddle, second = tables()
    code = (depth_owner * B_OWN + depth_slot) * 128 + intersection
    code = jnp.pad(code.T.reshape(12, 128), ((0, 4), (0, 0)))
    scale = jnp.tile((taper * (1.0 / math.sqrt(NT))).reshape(32, 32), (1, 8))
    vmem = pl.BlockSpec(memory_space=pltpu.VMEM)
    dma = pltpu.SemaphoreType.DMA
    got = pl.pallas_call(
        kernel,
        out_shape=jax.ShapeDtypeStruct((8 * N_TM, 128), F32),
        in_specs=[pl.BlockSpec(memory_space=pl.ANY)] + [vmem] * 5,
        out_specs=vmem,
        scratch_shapes=[
            pltpu.VMEM((N_CHAN, TC, CH), BF),
            pltpu.VMEM((N_CHAN, 16, 128), jnp.int32),
            pltpu.VMEM((NX * B_OWN, 128), F32),
            pltpu.VMEM((NX, 128, 128), F32),
            pltpu.VMEM((NX, 128, 128), F32),
            pltpu.VMEM((N_TM, 16, 128), F32),
            pltpu.VMEM((N_TM * 16, 128), F32),
            pltpu.VMEM((B_OWN, 1536), BF),
            pltpu.VMEM((8 * N_TM, 128), F32),
            pltpu.VMEM((8 * N_TM, 128), F32),
        ]
        + [dma((8,))] * 8
        + [dma((4,)), dma((4,)), dma, dma, dma, dma, dma((2,))],
        compiler_params=pltpu.CompilerParams(
            collective_id=0, has_side_effects=True, vmem_limit_bytes=48 * 2**20
        ),
        name="stack_and_transform",
    )(raw, code, jnp.asarray(first), jnp.asarray(twiddle), jnp.asarray(second), scale)
    got = got.reshape(N_TM, 8, 128)[:, :4].reshape(N_TM, 2, 8, 32)
    return got.transpose(1, 0, 2, 3).reshape(2, B_OWN, 32)


def solution(mesh):
    return jax.shard_map(
        local,
        mesh=mesh,
        in_specs=(P("tm", "chan"), P(), P("chan", None), P("chan", None), P("chan", None)),
        out_specs=P(None, "chan", "tm"),
        check_vma=False,
    )
```

time: 314 us -> 63.5 us (0.20); the launches traced: 310 us -> 62.8 us
  waiting for transfers between devices: 175 us -> 0 us
  blocking collectives: 65.2 us -> 0 us
  Pallas kernels: 0 us -> 57.7 us
  starting transfers between devices: 30.7 us -> 0 us
  between operations: 13.6 us -> 0.07 us
  local copies, waits for them, and re-layouts: 13.1 us -> 3.57 us
  other arithmetic: 8.11 us -> 1.47 us
  matrix products: 3.95 us -> 0 us
    reduce_scatter x1 -> x0, waiting for transfers between devices: 149 us -> none  [local(): lax.psum_scatter(partial_stack, 'tm', scatter_dimension=2, tiled=True)]
    psum x1 -> x0, blocking collectives: 65.2 us -> none  [local(): weight_total = lax.psum(weight_sum, 'tm')]
    pallas_call x0 -> x1, Pallas kernels: none -> 57.7 us  [local(): pl.pallas_call(kernel, out_shape=jax.ShapeDtypeStruct((8 * N_TM, 128), F3...]
    all_to_all x3 -> x0, starting transfers between devices: 30.7 us -> none  [the longest x1 16.5 us: local(): lax.all_to_all(grouped, 'tm', split_axis=1, concat_axis=0, tiled=True)]
    all_to_all x3 -> x0, waiting for transfers between devices: 25.9 us -> none  [the longest x1 15.7 us: local(): lax.all_to_all(outgoing, 'chan', split_axis=0, concat_axis=0, tiled=True)]
    reshape x9 -> x4, local copies, waits for them, and re-layouts: 7.62 us -> 0.9 us  [the longest x2 0.76 us: local(): return got.transpose(1, 0, 2, 3).reshape(2, B_OWN, 32)]
    dot_general x6 -> x0, matrix products: 3.95 us -> none  [the longest x1 0.73 us: spectrum_rows(): jnp.dot(jnp.sin(angle_one), samples, precision=HIGHEST)]
    scatter-add x2 -> x0, other arithmetic: 3.47 us -> none  [the longest x1 2.26 us: stack_bins(): stack_sum = jax.ops.segment_sum(arrived_rows, bin_index, num_segments=B_OWN)]
  transfers between devices with their start and end apart: 4 -> 0, of which waited for: 3 -> 0; matrix products, arithmetic and copies ran while one was open for 6% -> 0% of each run, Pallas kernels for 0% -> 0%
where the time goes in v1:
time: 63.5 us; the launch traced here: 62.8 us
  Pallas kernels  57.7 us (91%)
  local copies, waits for them, and re-layouts  3.57 us (6%)
  other arithmetic  1.47 us (2%)
    pallas_call x1, Pallas kernels, local(): pl.pallas_call(kernel, out_shape=jax.ShapeDtypeStruct((8 * N_TM, 128), F3...  57.7 us
    unnamed x8, local copies, waits for them, and re-layouts  2.48 us

profile of v1, /device:TPU:1, one launch (start us, length us, event | category | flops | bytes accessed | tf_op | source)
XLA Modules:
  0.0 62.8 jit_solution(4268962631703261876)
XLA Ops:
  0.0 0.0 copy-start
  0.0 0.7 %broadcast_multiply_fusion = f32[1024]{0:T(1024)S(1)} fusion(f32[1024]{0:T(1024)} %param.9), kind=kLoop, calls=%fused_computation.2 | loop fusion | flops 1024 | bytes 8192 | tf_op jit(solution)/shard_map/mul | solution.py:290
  0.7 0.7 %add_bitcast_fusion = s32[2,768]{1,0:T(2,128)S(1)} fusion(s32[768,2]{0,1:T(2,128)} %param.12, s32[768,2]{0,1:T(2,128)} %param.11, s32[768,2]{0,1:T(2,128)} %param.10), kind=kLoop, calls=%fused_computation.1 | loop fusion | flops 6144 | bytes 24576 | tf_op jit(solution)/shard_map/transpose | solution.py:289
  1.5 0.1 tile.10
  1.6 0.1 tile.12.taper
  1.7 0.0 copy-done
  1.7 0.0 copy-start.1
  1.7 0.9 %copy-done.1 = bf16[64,1536]{1,0:T(8,128)(2,1)S(1)} copy-done((bf16[64,1536]{1,0:T(8,128)(2,1)S(1)}, bf16[64,1536]{1,0:T(8,128)(2,1)}, u32[]{:S(2)}) %copy-start.1) | copy-done | bytes 196632
  2.6 0.0 copy-start.2
  2.6 0.8 %copy-done.2 = f32[2,32,256]{2,1,0:T(8,128)S(1)} copy-done((f32[2,32,256]{2,1,0:T(8,128)S(1)}, f32[2,32,256]{2,1,0:T(8,128)}, u32[]{:S(2)}) %copy-start.2) | copy-done | bytes 65560
  3.5 0.0 copy-start.3
  3.5 0.7 %copy-done.3 = bf16[64,96]{1,0:T(8,128)(2,1)S(1)} copy-done((bf16[64,96]{1,0:T(8,128)(2,1)S(1)}, bf16[64,96]{1,0:T(8,128)(2,1)}, u32[]{:S(2)}) %copy-start.3) | copy-done | bytes 12312
  4.2 57.7 %stack_and_transform.1 = f32[256,128]{1,0:T(8,128)S(1)} custom-call(bf16[256,768]{1,0:T(8,128)(2,1)S(1)} %copy-done, s32[16,128]{1,0:T(8,128)S(1)} %pad.4.code, bf16[64,96]{1,0:T(8,128)(2,1)S(1)} %copy-done.3, f32[2,32,256]{2,1,0:T(8,128)S(1)} %copy-done.2, bf16[64,1536]{1,0:T(8,128)(2,1)S(1)} %copy-done.1, f32[32,256]{1,0:T(8,128)S(1)} %tile.12.taper), custom_call_target="tpu_custom_call" | custom-call | tf_op jit(solution)/shard_map/stack_and_transform/pallas_call | solution.py:293
  61.9 0.1 reshape.18
  62.1 0.7 %copy.12 = f32[2,256,32]{1,2,0:T(8,128)} copy(f32[2,256,32]{2,1,0:T(8,128)S(1)} %copy_bitcast_fusion) | data formatting | bytes 131072 | tf_op jit(solution)/shard_map/reshape | solution.py:318
  (5 shorter events, 0.1 us)
Async XLA Ops:
  0.0 1.7 %copy-start = (bf16[256,768]{1,0:T(8,128)(2,1)S(1)}, bf16[256,768]{1,0:T(8,128)(2,1)}, u32[]{:S(2)}) copy-start(bf16[256,768]{1,0:T(8,128)(2,1)} %raw.1) | copy-start | bytes 1179652
  1.7 0.9 %copy-start.1 = (bf16[64,1536]{1,0:T(8,128)(2,1)S(1)}, bf16[64,1536]{1,0:T(8,128)(2,1)}, u32[]{:S(2)}) copy-start(bf16[64,1536]{1,0:T(8,128)(2,1)} %constant.16.clone.second) | copy-start | bytes 589828
  2.6 0.8 %copy-start.2 = (f32[2,32,256]{2,1,0:T(8,128)S(1)}, f32[2,32,256]{2,1,0:T(8,128)}, u32[]{:S(2)}) copy-start(f32[2,32,256]{2,1,0:T(8,128)} %constant.15.clone.twiddle) | copy-start | bytes 196612
  3.5 0.7 %copy-start.3 = (bf16[64,96]{1,0:T(8,128)(2,1)S(1)}, bf16[64,96]{1,0:T(8,128)(2,1)}, u32[]{:S(2)}) copy-start(bf16[64,96]{1,0:T(8,128)(2,1)} %constant.14.clone.first) | copy-start | bytes 36868

commit v2 on v0

v2 whole, which is shorter than its diff:
```python
import math

import jax
import jax.numpy as jnp
import numpy as np
from jax import lax
from jax.experimental import pallas as pl
from jax.experimental.pallas import tpu as pltpu
from jax.sharding import PartitionSpec as P

NT = 8192
KLO = 128
NB = 1024
N_TM = 32
N_CHAN = 16
NX = 4
CH = 768
TB = 256
TC = 16
BF = jnp.bfloat16
F32 = jnp.float32
MESH = pl.DeviceIdType.MESH


def split_np(a):
    hi = a.astype(jnp.bfloat16)
    lo = (a - hi.astype(np.float64)).astype(jnp.bfloat16)
    return hi, lo


def tables():
    p = np.arange(32)
    s = np.arange(TB)
    ang = 2.0 * np.pi * (np.outer(p, p) % 32) / 32
    first = np.concatenate([np.cos(ang), -np.sin(ang)], 0)
    hi, lo = split_np(first)
    first = np.concatenate([hi, hi, lo], 1)
    first = np.concatenate([first, np.zeros((64, 32), first.dtype)], 1)
    mid = 2.0 * np.pi * np.outer(p, s) / NT
    twiddle = np.concatenate([np.cos(mid), np.sin(mid)]).astype(np.float32)
    q = KLO // 32 + np.arange(NB // 32)
    ang = 2.0 * np.pi * (np.outer(q, s) % TB) / TB
    c, z = np.cos(ang), np.sin(ang)
    second = np.concatenate([np.concatenate([c, z], 1), np.concatenate([-z, c], 1)], 0)
    hi, lo = split_np(second)
    second = np.concatenate([hi, hi, lo], 1)
    return first, twiddle, second


def split(a):
    hi = a.astype(BF)
    lo = (a - hi.astype(F32)).astype(BF)
    return hi, lo


def kernel(
    raw, owner_in, slot_in, weight_in, first_in, twiddle_in, second_in, taper_in, out,
    owner, slot, weight, first, twiddle, second, taper, scale,
    blocks, codes, acc, sums, parts, rows, samples, mid, outgo, arrived,
    send_raw, recv_raw, send_code, recv_code, send_x, recv_x,
    send_t, recv_t, send_f, recv_f, index_sem, table_sem, own_sem,
):
    me = lax.axis_index("tm")
    g = lax.axis_index("chan")
    core, x, zl = lax.rem(g, 2), lax.rem(g // 2, NX), g // 8
    y, zh = lax.rem(me, 8), me // 8

    index_copies = [
        pltpu.make_async_copy(a, b, index_sem.at[k])
        for k, (a, b) in enumerate([(owner_in, owner), (slot_in, slot), (weight_in, weight)])
    ]
    table_copies = [
        pltpu.make_async_copy(a, b, table_sem.at[k])
        for k, (a, b) in enumerate(
            [(taper_in, taper), (first_in, first), (twiddle_in, twiddle), (second_in, second)]
        )
    ]
    for copy in index_copies:
        copy.start()

    def relative(k):
        step = k // 4
        dx = step + jnp.where(step == 2, 1, jnp.where(step == 3, -1, 0))
        return lax.rem(k // 2, 2), dx, lax.rem(k, 2)

    def to_chan(k):
        dz, dx, dc = relative(k)
        return (lax.rem(zl + dz, 2) * NX + lax.rem(x + dx, NX)) * 2 + lax.rem(core + dc, 2)

    def from_chan(k):
        dz, dx, dc = relative(k)
        return (lax.rem(zl + dz, 2) * NX + lax.rem(x + NX - dx, NX)) * 2 + lax.rem(core + dc, 2)

    def to_tm(n):
        far, m = n // 4, lax.rem(n, 4)
        dy = 4 + jnp.where(lax.rem(far, 2) == 1, -((far + 1) // 2), far // 2)
        dz = jnp.where(m == 0, 2, jnp.where(m == 1, 1, jnp.where(m == 2, 3, 0)))
        return lax.rem(zh + dz, 4) * 8 + lax.rem(y + dy, 8)

    barrier = pltpu.get_barrier_semaphore()

    def greet_tm(n, _):
        pl.semaphore_signal(barrier, inc=1, device_id=(to_tm(n), g), device_id_type=MESH)
        return 0

    def greet_chan(k, _):
        pl.semaphore_signal(barrier, inc=1, device_id=(me, to_chan(k)), device_id_type=MESH)
        return 0

    lax.fori_loop(0, N_TM - 1, greet_tm, 0)
    lax.fori_loop(1, N_CHAN, greet_chan, 0)

    def chunk(i):
        return pl.ds(pl.multiple_of(i * TC, TC), TC)

    own_raw = pltpu.make_async_copy(raw.at[chunk(g), :], blocks.at[g], own_sem)
    own_raw.start()
    for copy in table_copies:
        copy.start()
    for copy in index_copies:
        copy.wait()
    code = (owner[...] * 256 + slot[...]) * 128 + weight[...]
    for j in range(2):
        for m in range(CH // 128):
            r = 6 * j + m
            codes[g, r // 4, pl.ds(r % 4, 1), :] = code[j : j + 1, 128 * m : 128 * m + 128]
    acc[...] = jnp.zeros_like(acc)
    pl.semaphore_wait(barrier, N_TM - 1 + N_CHAN - 1)

    def raw_copy(k):
        to = to_chan(k)
        return pltpu.make_async_remote_copy(
            src_ref=raw.at[chunk(to), :], dst_ref=blocks.at[g],
            send_sem=send_raw.at[k], recv_sem=recv_raw.at[k],
            device_id=(me, to), device_id_type=MESH,
        )

    def code_copy(k):
        return pltpu.make_async_remote_copy(
            src_ref=codes.at[g], dst_ref=codes.at[g],
            send_sem=send_code.at[k], recv_sem=recv_code.at[k],
            device_id=(me, to_chan(k)), device_id_type=MESH,
        )

    def send_group(n, _):
        k = N_CHAN - 1 - n
        code_copy(k).start()
        raw_copy(k).start()
        return 0

    lax.fori_loop(0, N_CHAN - 1, send_group, 0)

    row = lax.broadcasted_iota(jnp.int32, (256, 128), 0).astype(F32).astype(BF)

    def process(src):
        total = None
        for m2 in range(CH // 256):
            data = [blocks[src, :, pl.ds(256 * m2 + 128 * n, 128)] for n in range(2)]
            for j in range(2):
                left, right = [], []
                for n in range(2):
                    r = 6 * j + 2 * m2 + n
                    c = codes[src, r // 4, pl.ds(r % 4, 1), :]

                    def spread(v):
                        return jnp.broadcast_to(v.astype(F32), (16, 128)).astype(BF)

                    key, low, w = spread(c >> 11), spread((c >> 7) & 15), spread(c & 127)
                    key = jnp.concatenate([key] * 16, 0)
                    w = jnp.concatenate([w] * 16, 0)
                    left.append(jnp.where(row == key, w, BF(0)))
                    right.append(
                        jnp.concatenate(
                            [jnp.where(low == BF(v), data[n], BF(0)) for v in range(16)], 0
                        )
                    )
                part = lax.dot_general(
                    jnp.concatenate(left, 1), jnp.concatenate(right, 1),
                    (((1,), (1,)), ((), ())), preferred_element_type=F32,
                )
                total = part if total is None else total + part
        acc[...] += total

    own_raw.wait()
    process(g)

    def step(k, _):
        code_copy(k).wait_recv()
        raw_copy(k).wait_recv()
        process(from_chan(k))
        return 0

    lax.fori_loop(1, N_CHAN, step, 0)
    for h in range(2):
        sums[:, pl.ds(16 * h, 16), :] = acc[:, pl.ds(128 * h, 128)].reshape(16, 16, 128)

    def part(i):
        return pl.ds(pl.multiple_of(i * 32, 32), 32)

    def x_copy(k):
        to = to_chan(k)
        return pltpu.make_async_remote_copy(
            src_ref=sums.at[to], dst_ref=parts.at[part(g), :],
            send_sem=send_x.at[k], recv_sem=recv_x.at[k],
            device_id=(me, to), device_id_type=MESH,
        )

    def send_part(n, _):
        x_copy(N_CHAN - 1 - n).start()
        return 0

    def wait_part(k, _):
        x_copy(k).wait_recv()
        return 0

    lax.fori_loop(0, N_CHAN - 1, send_part, 0)
    parts[part(g), :] = sums[g]
    for copy in table_copies:
        copy.wait()
    quarter = lax.broadcasted_iota(jnp.int32, (8, 128), 1) // 32
    t = taper[...] * (1.0 / math.sqrt(NT))
    for j in range(4):
        line = jnp.zeros((8, 128), F32)
        for n in range(4):
            moved = pltpu.roll(t, (32 * (n - j)) % 128, 1) if n != j else t
            line = jnp.where(quarter == n, moved, line)
        scale[pl.ds(j, 8, 4), :] = line
    every = codes[...].reshape(N_CHAN * 3, 4, 128)
    inverse = []
    for b in range(8):
        hit = jnp.where((every >> 7) == g * 256 + me * 8 + b, every & 127, 0)
        total = jnp.sum(hit, axis=0).astype(F32)
        total = jnp.sum(jnp.sum(total, axis=0, keepdims=True), axis=1, keepdims=True)
        inverse.append(1.0 / jnp.maximum(total, 1.0))
    lax.fori_loop(1, N_CHAN, wait_part, 0)
    for i in range(N_TM):
        rows[i] = parts[pl.ds((i % 2) * 16 + i // 2, 16, 32), :]

    def send_rows(n, _):
        to = to_tm(n)
        pltpu.make_async_remote_copy(
            src_ref=rows.at[to], dst_ref=samples.at[chunk(me), :],
            send_sem=send_t, recv_sem=recv_t, device_id=(to, g), device_id_type=MESH,
        ).start()
        return 0

    lax.fori_loop(0, N_TM - 1, send_rows, 0)
    samples[chunk(me), :] = rows[me]
    all_t = pltpu.make_async_remote_copy(
        src_ref=samples.at[pl.ds(0, 16 * (N_TM - 1)), :],
        dst_ref=samples.at[pl.ds(0, 16 * (N_TM - 1)), :],
        send_sem=send_t, recv_sem=recv_t, device_id=(to_tm(0), g), device_id_type=MESH,
    )
    all_t.wait_recv()

    lane = lax.broadcasted_iota(jnp.int32, (N_TM, 128), 1) // 16
    halves = []
    for u in range(2):
        v = [samples[pl.ds(8 * u + n, N_TM, 16), :] for n in range(8)]
        for bit in (1, 2, 4):
            low = (lane & bit) == 0
            w = list(v)
            for n in range(8):
                if n & bit == 0:
                    w[n] = jnp.where(low, v[n], pltpu.roll(v[n + bit], 16 * bit, 1))
                    w[n + bit] = jnp.where(low, pltpu.roll(v[n], 128 - 16 * bit, 1), v[n + bit])
            v = w
        halves.append(v)
    cos, sin = twiddle[pl.ds(0, 32), :], twiddle[pl.ds(32, 32), :]
    for b in range(8):
        hi, lo = split(jnp.concatenate([halves[0][b], halves[1][b]], 1) * inverse[b])
        here = jnp.concatenate([hi, lo, hi, jnp.zeros_like(hi)], 0)
        f = jnp.dot(first[...], here, preferred_element_type=F32)
        re, im = f[:32], f[32:]
        z = jnp.concatenate([re * cos + im * sin, im * cos - re * sin], 1)
        hi, lo = split(z)
        mid[pl.ds(32 * b, 32), pl.ds(0, 512)] = hi
        mid[pl.ds(32 * b, 32), pl.ds(512, 512)] = lo
        mid[pl.ds(32 * b, 32), pl.ds(1024, 512)] = hi
    spec = lax.dot_general(
        second[...], mid[...], (((1,), (1,)), ((), ())), preferred_element_type=F32
    )
    for r in range(2):
        for h in range(2):
            band = spec[32 * r : 32 * r + 32, 128 * h : 128 * h + 128] * scale[...]
            outgo[:, 2 * r + h, :] = band

    def send_band(n, _):
        to = to_tm(n)
        pltpu.make_async_remote_copy(
            src_ref=outgo.at[to], dst_ref=arrived.at[me],
            send_sem=send_f, recv_sem=recv_f, device_id=(to, g), device_id_type=MESH,
        ).start()
        return 0

    lax.fori_loop(0, N_TM - 1, send_band, 0)
    arrived[me] = outgo[me]
    all_f = pltpu.make_async_remote_copy(
        src_ref=arrived.at[pl.ds(0, N_TM - 1)], dst_ref=arrived.at[pl.ds(0, N_TM - 1)],
        send_sem=send_f, recv_sem=recv_f, device_id=(to_tm(0), g), device_id_type=MESH,
    )
    all_f.wait_recv()
    out[...] = arrived[...]

    def drain(k, _):
        code_copy(k).wait_send()
        raw_copy(k).wait_send()
        x_copy(k).wait_send()
        return 0

    lax.fori_loop(1, N_CHAN, drain, 0)
    all_t.wait_send()
    all_f.wait_send()


def local(raw, taper, depth_owner, depth_slot, intersection):
    first, twiddle, second = tables()
    anywhere = pl.BlockSpec(memory_space=pl.ANY)
    dma = pltpu.SemaphoreType.DMA
    vmem = pltpu.VMEM
    got = pl.pallas_call(
        kernel,
        out_shape=jax.ShapeDtypeStruct((N_TM, 4, 128), F32),
        in_specs=[anywhere] * 8,
        out_specs=pl.BlockSpec(memory_space=pltpu.VMEM),
        scratch_shapes=[
            vmem((2, CH), jnp.int32),
            vmem((2, CH), jnp.int32),
            vmem((2, CH), jnp.int32),
            vmem((64, 128), BF),
            vmem((64, TB), F32),
            vmem((64, 1536), BF),
            vmem((8, 128), F32),
            vmem((32, 128), F32),
            vmem((N_CHAN, TC, CH), BF),
            vmem((N_CHAN, 3, 4, 128), jnp.int32),
            vmem((256, 256), F32),
            vmem((N_CHAN, 32, 128), F32),
            vmem((N_CHAN * 32, 128), F32),
            vmem((N_TM, 16, 128), F32),
            vmem((N_TM * 16, 128), F32),
            vmem((256, 1536), BF),
            vmem((N_TM, 4, 128), F32),
            vmem((N_TM, 4, 128), F32),
        ]
        + [dma((N_CHAN,))] * 6
        + [dma, dma, dma, dma, dma((3,)), dma((4,)), dma],
        compiler_params=pltpu.CompilerParams(
            collective_id=0, has_side_effects=True, vmem_limit_bytes=60 * 2**20
        ),
        name="stack_and_transform",
    )(
        raw, depth_owner.T, depth_slot.T, intersection.T,
        jnp.asarray(first), jnp.asarray(twiddle), jnp.asarray(second), taper.reshape(8, 128),
    )
    got = got.reshape(N_TM, 2, 8, 32)
    return got.transpose(1, 0, 2, 3).reshape(2, 256, 32)


def solution(mesh):
    return jax.shard_map(
        local,
        mesh=mesh,
        in_specs=(P("tm", "chan"), P(), P("chan", None), P("chan", None), P("chan", None)),
        out_specs=P(None, "chan", "tm"),
        check_vma=False,
    )
```

time: 314 us -> 55.6 us (0.18); the launches traced: 310 us -> 55.4 us
  waiting for transfers between devices: 175 us -> 0 us
  blocking collectives: 65.2 us -> 0 us
  Pallas kernels: 0 us -> 53.7 us
  starting transfers between devices: 30.7 us -> 0 us
  between operations: 13.6 us -> 0.02 us
  local copies, waits for them, and re-layouts: 13.1 us -> 1.73 us
  other arithmetic: 8.11 us -> 0 us
  matrix products: 3.95 us -> 0 us
    reduce_scatter x1 -> x0, waiting for transfers between devices: 149 us -> none  [local(): lax.psum_scatter(partial_stack, 'tm', scatter_dimension=2, tiled=True)]
    psum x1 -> x0, blocking collectives: 65.2 us -> none  [local(): weight_total = lax.psum(weight_sum, 'tm')]
    pallas_call x0 -> x1, Pallas kernels: none -> 53.7 us  [local(): pl.pallas_call(kernel, out_shape=jax.ShapeDtypeStruct((N_TM, 4, 128), F32...]
    all_to_all x3 -> x0, starting transfers between devices: 30.7 us -> none  [the longest x1 16.5 us: local(): lax.all_to_all(grouped, 'tm', split_axis=1, concat_axis=0, tiled=True)]
    all_to_all x3 -> x0, waiting for transfers between devices: 25.9 us -> none  [the longest x1 15.7 us: local(): lax.all_to_all(outgoing, 'chan', split_axis=0, concat_axis=0, tiled=True)]
    reshape x9 -> x3, local copies, waits for them, and re-layouts: 7.62 us -> 1.73 us  [the longest x2 0.99 us: local(): got = got.reshape(N_TM, 2, 8, 32)]
    dot_general x6 -> x0, matrix products: 3.95 us -> none  [the longest x1 0.73 us: spectrum_rows(): jnp.dot(jnp.sin(angle_one), samples, precision=HIGHEST)]
    scatter-add x2 -> x0, other arithmetic: 3.47 us -> none  [the longest x1 2.26 us: stack_bins(): stack_sum = jax.ops.segment_sum(arrived_rows, bin_index, num_segments=B_OWN)]
  transfers between devices with their start and end apart: 4 -> 0, of which waited for: 3 -> 0; matrix products, arithmetic and copies ran while one was open for 6% -> 0% of each run, Pallas kernels for 0% -> 0%
where the time goes in v2:
time: 55.6 us; the launch traced here: 55.4 us
  Pallas kernels  53.7 us (97%)
  local copies, waits for them, and re-layouts  1.73 us (3%)
    pallas_call x1, Pallas kernels, local(): pl.pallas_call(kernel, out_shape=jax.ShapeDtypeStruct((N_TM, 4, 128), F32...  53.7 us

profile of v2, /device:TPU:1, one launch (start us, length us, event | category | flops | bytes accessed | tf_op | source)
XLA Modules:
  0.0 55.4 jit_solution(18362366194887016382)
XLA Ops:
  0.0 53.7 %stack_and_transform.1 = f32[32,4,128]{2,1,0:T(4,128)} custom-call(bf16[256,768]{1,0:T(8,128)(2,1)} %raw.1, s32[2,768]{1,0:T(2,128)} %bitcast.10, s32[2,768]{1,0:T(2,128)} %bitcast.11, s32[2,768]{1,0:T(2,128)} %bitcast.12, bf16[64,128]{1,0:T(8,128)(2,1)} %constant.6.clone.first_in, f32[64,256]{1,0:T(8,128)} %constant.7.clone.twiddle_in, ...), custom_call_target="tpu_custom_call" | custom-call | tf_op jit(solution)/shard_map/stack_and_transform/pallas_call | solution.py:321
  53.7 1.0 %reshape.10 = f32[32,2,8,32]{3,2,1,0:T(8,128)S(1)} reshape(f32[32,4,128]{2,1,0:T(4,128)} %stack_and_transform.1) | data formatting | bytes 131072 | tf_op jit(solution)/shard_map/reshape | solution.py:356
  54.7 0.7 %copy.11 = f32[2,256,32]{1,2,0:T(8,128)} copy(f32[2,256,32]{2,1,0:T(8,128)S(1)} %bitcast.9) | data formatting | bytes 131072 | tf_op jit(solution)/shard_map/reshape | solution.py:357
  (1 shorter events, 0.0 us)

commit v3 on v2

--- a/solution.py
+++ b/solution.py
@@ -58,7 +58,7 @@
     owner, slot, weight, first, twiddle, second, taper, scale,
     blocks, codes, acc, sums, parts, rows, samples, mid, outgo, arrived,
     send_raw, recv_raw, send_code, recv_code, send_x, recv_x,
-    send_t, recv_t, send_f, recv_f, index_sem, table_sem, own_sem,
+    send_t, recv_t, send_f, recv_f, index_sem, table_sem, own_sem, ring_sem,
 ):
     me = lax.axis_index("tm")
     g = lax.axis_index("chan")
@@ -99,15 +99,28 @@
 
     barrier = pltpu.get_barrier_semaphore()
 
-    def greet_tm(n, _):
-        pl.semaphore_signal(barrier, inc=1, device_id=(to_tm(n), g), device_id_type=MESH)
+    def along_y(d):
+        return zh * 8 + lax.rem(y + d, 8)
+
+    def greet_y(d, _):
+        pl.semaphore_signal(barrier, inc=1, device_id=(along_y(d), g), device_id_type=MESH)
+        return 0
+
+    def greet_z(d, _):
+        to = lax.rem(zh + d, 4) * 8 + y
+        pl.semaphore_signal(barrier, inc=1, device_id=(to, g), device_id_type=MESH)
+        return 0
+
+    def tell_y(d, _):
+        pl.semaphore_signal(ring_sem, inc=1, device_id=(along_y(d), g), device_id_type=MESH)
         return 0
 
     def greet_chan(k, _):
         pl.semaphore_signal(barrier, inc=1, device_id=(me, to_chan(k)), device_id_type=MESH)
         return 0
 
-    lax.fori_loop(0, N_TM - 1, greet_tm, 0)
+    lax.fori_loop(1, 8, greet_y, 0)
+    lax.fori_loop(1, 4, greet_z, 0)
     lax.fori_loop(1, N_CHAN, greet_chan, 0)
 
     def chunk(i):
@@ -125,7 +138,7 @@
             r = 6 * j + m
             codes[g, r // 4, pl.ds(r % 4, 1), :] = code[j : j + 1, 128 * m : 128 * m + 128]
     acc[...] = jnp.zeros_like(acc)
-    pl.semaphore_wait(barrier, N_TM - 1 + N_CHAN - 1)
+    pl.semaphore_wait(barrier, 7 + 3 + N_CHAN - 1)
 
     def raw_copy(k):
         to = to_chan(k)
@@ -143,12 +156,13 @@
         )
 
     def send_group(n, _):
-        k = N_CHAN - 1 - n
+        k = n + 1
         code_copy(k).start()
         raw_copy(k).start()
         return 0
 
     lax.fori_loop(0, N_CHAN - 1, send_group, 0)
+    lax.fori_loop(1, 8, tell_y, 0)
 
     row = lax.broadcasted_iota(jnp.int32, (256, 128), 0).astype(F32).astype(BF)
 
@@ -165,7 +179,9 @@
                     def spread(v):
                         return jnp.broadcast_to(v.astype(F32), (16, 128)).astype(BF)
 
-                    key, low, w = spread(c >> 11), spread((c >> 7) & 15), spread(c & 127)
+                    key = spread(((c >> 15) << 4) + ((c >> 7) & 15))
+                    low = spread(((c >> 11) & 1) * 8 + ((c >> 12) & 7))
+                    w = spread(c & 127)
                     key = jnp.concatenate([key] * 16, 0)
                     w = jnp.concatenate([w] * 16, 0)
                     left.append(jnp.where(row == key, w, BF(0)))
@@ -228,13 +244,13 @@
     every = codes[...].reshape(N_CHAN * 3, 4, 128)
     inverse = []
     for b in range(8):
-        hit = jnp.where((every >> 7) == g * 256 + me * 8 + b, every & 127, 0)
+        hit = jnp.where((every >> 7) == g * 256 + b * 32 + me, every & 127, 0)
         total = jnp.sum(hit, axis=0).astype(F32)
         total = jnp.sum(jnp.sum(total, axis=0, keepdims=True), axis=1, keepdims=True)
         inverse.append(1.0 / jnp.maximum(total, 1.0))
     lax.fori_loop(1, N_CHAN, wait_part, 0)
     for i in range(N_TM):
-        rows[i] = parts[pl.ds((i % 2) * 16 + i // 2, 16, 32), :]
+        rows[i] = parts[pl.ds(i, 16, 32), :]
 
     def send_rows(n, _):
         to = to_tm(n)
@@ -244,6 +260,7 @@
         ).start()
         return 0
 
+    pl.semaphore_wait(ring_sem, 7)
     lax.fori_loop(0, N_TM - 1, send_rows, 0)
     samples[chunk(me), :] = rows[me]
     all_t = pltpu.make_async_remote_copy(
@@ -300,7 +317,12 @@
         send_sem=send_f, recv_sem=recv_f, device_id=(to_tm(0), g), device_id_type=MESH,
     )
     all_f.wait_recv()
-    out[...] = arrived[...]
+    for r in range(2):
+        for h in range(2):
+            turned = arrived[:, 2 * r + h, :].T
+            out[r, :, pl.ds(128 * h, 128)] = jnp.concatenate(
+                [turned[32 * n : 32 * n + 32] for n in range(4)], 1
+            )
 
     def drain(k, _):
         code_copy(k).wait_send()
@@ -320,7 +342,7 @@
     vmem = pltpu.VMEM
     got = pl.pallas_call(
         kernel,
-        out_shape=jax.ShapeDtypeStruct((N_TM, 4, 128), F32),
+        out_shape=jax.ShapeDtypeStruct((2, 32, 256), F32),
         in_specs=[anywhere] * 8,
         out_specs=pl.BlockSpec(memory_space=pltpu.VMEM),
         scratch_shapes=[
@@ -344,7 +366,7 @@
             vmem((N_TM, 4, 128), F32),
         ]
         + [dma((N_CHAN,))] * 6
-        + [dma, dma, dma, dma, dma((3,)), dma((4,)), dma],
+        + [dma, dma, dma, dma, dma((3,)), dma((4,)), dma, pltpu.SemaphoreType.REGULAR],
         compiler_params=pltpu.CompilerParams(
             collective_id=0, has_side_effects=True, vmem_limit_bytes=60 * 2**20
         ),
@@ -353,8 +375,7 @@
         raw, depth_owner.T, depth_slot.T, intersection.T,
         jnp.asarray(first), jnp.asarray(twiddle), jnp.asarray(second), taper.reshape(8, 128),
     )
-    got = got.reshape(N_TM, 2, 8, 32)
-    return got.transpose(1, 0, 2, 3).reshape(2, 256, 32)
+    return got.transpose(0, 2, 1)
 
 
 def solution(mesh):

time: 55.6 us -> 50.8 us (0.914)
  Pallas kernels: 53.7 us -> 49.2 us
    pallas_call x1, Pallas kernels: 53.7 us -> 49.2 us  [local(): pl.pallas_call(kernel, out_shape=jax.ShapeDtypeStruct((2, 32, 256), F32),...]
    reshape x3 -> x0, local copies, waits for them, and re-layouts: 1.73 us -> none  [the longest x2 0.99 us: local(): got = got.reshape(N_TM, 2, 8, 32)]
    unnamed x0 -> x1, local copies, waits for them, and re-layouts: none -> 1.47 us
where the time goes in v3:
time: 50.8 us; the launch traced here: 50.6 us
  Pallas kernels  49.2 us (97%)
  local copies, waits for them, and re-layouts  1.47 us (3%)
    pallas_call x1, Pallas kernels, local(): pl.pallas_call(kernel, out_shape=jax.ShapeDtypeStruct((2, 32, 256), F32),...  49.2 us
    unnamed x1, local copies, waits for them, and re-layouts  1.47 us

profile of v3, /device:TPU:1, one launch (start us, length us, event | category | flops | bytes accessed | tf_op | source)
XLA Modules:
  0.0 50.6 jit_solution(11716877735876107942)
XLA Ops:
  0.0 49.2 %stack_and_transform.1 = f32[2,32,256]{2,1,0:T(8,128)} custom-call(bf16[256,768]{1,0:T(8,128)(2,1)} %raw.1, s32[2,768]{1,0:T(2,128)} %bitcast.6, s32[2,768]{1,0:T(2,128)} %bitcast.7, s32[2,768]{1,0:T(2,128)} %bitcast.8, bf16[64,128]{1,0:T(8,128)(2,1)} %constant.6.clone.first_in, f32[64,256]{1,0:T(8,128)} %constant.7.clone.twiddle_in, ...), custom_call_target="tpu_custom_call" | custom-call | tf_op jit(solution)/shard_map/stack_and_transform/pallas_call | solution.py:343
  49.2 1.5 %copy.10 = f32[2,256,32]{1,2,0:T(8,128)} copy(f32[2,256,32]{1,2,0:T(8,128)} %bitcast.5) | data formatting | bytes 131072

commit v4 on v3

--- a/solution.py
+++ b/solution.py
@@ -91,6 +91,12 @@
         dz, dx, dc = relative(k)
         return (lax.rem(zl + dz, 2) * NX + lax.rem(x + NX - dx, NX)) * 2 + lax.rem(core + dc, 2)
 
+    def place_of(chan):
+        dz = lax.rem(chan // 8 + zl, 2)
+        dx = lax.rem(x + NX - (chan // 2) % NX, NX)
+        near = dx + jnp.where(dx == 2, 1, jnp.where(dx == 3, -1, 0))
+        return near * 4 + dz * 2 + lax.rem(chan % 2 + core, 2)
+
     def to_tm(n):
         far, m = n // 4, lax.rem(n, 4)
         dy = 4 + jnp.where(lax.rem(far, 2) == 1, -((far + 1) // 2), far // 2)
@@ -128,8 +134,6 @@
 
     own_raw = pltpu.make_async_copy(raw.at[chunk(g), :], blocks.at[g], own_sem)
     own_raw.start()
-    for copy in table_copies:
-        copy.start()
     for copy in index_copies:
         copy.wait()
     code = (owner[...] * 256 + slot[...]) * 128 + weight[...]
@@ -163,6 +167,8 @@
 
     lax.fori_loop(0, N_CHAN - 1, send_group, 0)
     lax.fori_loop(1, 8, tell_y, 0)
+    for copy in table_copies:
+        copy.start()
 
     row = lax.broadcasted_iota(jnp.int32, (256, 128), 0).astype(F32).astype(BF)
 
@@ -216,13 +222,13 @@
     def x_copy(k):
         to = to_chan(k)
         return pltpu.make_async_remote_copy(
-            src_ref=sums.at[to], dst_ref=parts.at[part(g), :],
+            src_ref=sums.at[to], dst_ref=parts.at[part(k), :],
             send_sem=send_x.at[k], recv_sem=recv_x.at[k],
             device_id=(me, to), device_id_type=MESH,
         )
 
     def send_part(n, _):
-        x_copy(N_CHAN - 1 - n).start()
+        x_copy(n + 1).start()
         return 0
 
     def wait_part(k, _):
@@ -230,7 +236,7 @@
         return 0
 
     lax.fori_loop(0, N_CHAN - 1, send_part, 0)
-    parts[part(g), :] = sums[g]
+    parts[pl.ds(0, 32), :] = sums[g]
     for copy in table_copies:
         copy.wait()
     quarter = lax.broadcasted_iota(jnp.int32, (8, 128), 1) // 32
@@ -248,21 +254,25 @@
         total = jnp.sum(hit, axis=0).astype(F32)
         total = jnp.sum(jnp.sum(total, axis=0, keepdims=True), axis=1, keepdims=True)
         inverse.append(1.0 / jnp.maximum(total, 1.0))
-    lax.fori_loop(1, N_CHAN, wait_part, 0)
-    for i in range(N_TM):
-        rows[i] = parts[pl.ds(i, 16, 32), :]
-
-    def send_rows(n, _):
-        to = to_tm(n)
-        pltpu.make_async_remote_copy(
-            src_ref=rows.at[to], dst_ref=samples.at[chunk(me), :],
-            send_sem=send_t, recv_sem=recv_t, device_id=(to, g), device_id_type=MESH,
-        ).start()
-        return 0
+
+    def send_rows(half):
+        def send(n, _):
+            to = to_tm(n)
+            rows[to, pl.ds(8 * half, 8), :] = parts[pl.ds(256 * half + to, 8, 32), :]
+            pltpu.make_async_remote_copy(
+                src_ref=rows.at[to, pl.ds(8 * half, 8), :],
+                dst_ref=samples.at[pl.ds(pl.multiple_of(me * 16 + 8 * half, 8), 8), :],
+                send_sem=send_t, recv_sem=recv_t, device_id=(to, g), device_id_type=MESH,
+            ).start()
+            return 0
+
+        lax.fori_loop(0, N_TM - 1, send, 0)
 
     pl.semaphore_wait(ring_sem, 7)
-    lax.fori_loop(0, N_TM - 1, send_rows, 0)
-    samples[chunk(me), :] = rows[me]
+    for half in range(2):
+        lax.fori_loop(max(1, 8 * half), 8 * half + 8, wait_part, 0)
+        send_rows(half)
+    samples[chunk(me), :] = parts[pl.ds(me, 16, 32), :]
     all_t = pltpu.make_async_remote_copy(
         src_ref=samples.at[pl.ds(0, 16 * (N_TM - 1)), :],
         dst_ref=samples.at[pl.ds(0, 16 * (N_TM - 1)), :],
@@ -273,7 +283,7 @@
     lane = lax.broadcasted_iota(jnp.int32, (N_TM, 128), 1) // 16
     halves = []
     for u in range(2):
-        v = [samples[pl.ds(8 * u + n, N_TM, 16), :] for n in range(8)]
+        v = [samples[pl.ds(place_of(8 * u + n), N_TM, 16), :] for n in range(8)]
         for bit in (1, 2, 4):
             low = (lane & bit) == 0
             w = list(v)

time: 50.8 us -> 50.2 us (0.988)
  Pallas kernels: 49.2 us -> 48.5 us
    pallas_call x1, Pallas kernels: 49.2 us -> 48.5 us  [local(): pl.pallas_call(kernel, out_shape=jax.ShapeDtypeStruct((2, 32, 256), F32),...]
where the time goes in v4:
time: 50.2 us; the launch traced here: 50 us
  Pallas kernels  48.5 us (97%)
  local copies, waits for them, and re-layouts  1.47 us (3%)
    pallas_call x1, Pallas kernels, local(): pl.pallas_call(kernel, out_shape=jax.ShapeDtypeStruct((2, 32, 256), F32),...  48.5 us
    unnamed x1, local copies, waits for them, and re-layouts  1.47 us

profile of v4, /device:TPU:1, one launch (start us, length us, event | category | flops | bytes accessed | tf_op | source)
XLA Modules:
  0.0 50.0 jit_solution(16011097328357114536)
XLA Ops:
  0.0 48.5 %stack_and_transform.1 = f32[2,32,256]{2,1,0:T(8,128)} custom-call(bf16[256,768]{1,0:T(8,128)(2,1)} %raw.1, s32[2,768]{1,0:T(2,128)} %bitcast.6, s32[2,768]{1,0:T(2,128)} %bitcast.7, s32[2,768]{1,0:T(2,128)} %bitcast.8, bf16[64,128]{1,0:T(8,128)(2,1)} %constant.6.clone.first_in, f32[64,256]{1,0:T(8,128)} %constant.7.clone.twiddle_in, ...), custom_call_target="tpu_custom_call" | custom-call | tf_op jit(solution)/shard_map/stack_and_transform/pallas_call | solution.py:353
  48.5 1.5 %copy.10 = f32[2,256,32]{1,2,0:T(8,128)} copy(f32[2,256,32]{1,2,0:T(8,128)} %bitcast.5) | data formatting | bytes 131072

commit v5 on v4

--- a/solution.py
+++ b/solution.py
@@ -79,9 +79,14 @@
         copy.start()
 
     def relative(k):
-        step = k // 4
-        dx = step + jnp.where(step == 2, 1, jnp.where(step == 3, -1, 0))
-        return lax.rem(k // 2, 2), dx, lax.rem(k, 2)
+        n = k - 4
+        if isinstance(k, int):
+            return (n // 2 % 2, 1 + 2 * (n % 2), n // 4) if 4 <= k < 12 else (k // 2 % 2, 2 * (k // 12), k % 2)
+        mid = (k >= 4) & (k < 12)
+        dx = jnp.where(mid, 1 + 2 * lax.rem(k, 2), 2 * (k // 12))
+        dz = lax.rem(k // 2, 2)
+        dc = jnp.where(mid, n // 4, lax.rem(k, 2))
+        return dz, dx, dc
 
     def to_chan(k):
         dz, dx, dc = relative(k)
@@ -94,10 +99,14 @@
     def place_of(chan):
         dz = lax.rem(chan // 8 + zl, 2)
         dx = lax.rem(x + NX - (chan // 2) % NX, NX)
-        near = dx + jnp.where(dx == 2, 1, jnp.where(dx == 3, -1, 0))
-        return near * 4 + dz * 2 + lax.rem(chan % 2 + core, 2)
+        dc = lax.rem(chan % 2 + core, 2)
+        straight = 6 * dx + dz * 2 + dc
+        return jnp.where(lax.rem(dx, 2) == 0, straight, 4 + dc * 4 + dz * 2 + dx // 2)
 
     def to_tm(n):
+        if isinstance(n, int):
+            dy, dz = (4, 3, 5, 2, 6, 1, 7, 0)[n // 4], (2, 1, 3, 0)[n % 4]
+            return lax.rem(zh + dz, 4) * 8 + lax.rem(y + dy, 8)
         far, m = n // 4, lax.rem(n, 4)
         dy = 4 + jnp.where(lax.rem(far, 2) == 1, -((far + 1) // 2), far // 2)
         dz = jnp.where(m == 0, 2, jnp.where(m == 1, 1, jnp.where(m == 2, 3, 0)))
@@ -165,7 +174,8 @@
         raw_copy(k).start()
         return 0
 
-    lax.fori_loop(0, N_CHAN - 1, send_group, 0)
+    for n in range(N_CHAN - 1):
+        send_group(n, 0)
     lax.fori_loop(1, 8, tell_y, 0)
     for copy in table_copies:
         copy.start()
@@ -235,7 +245,8 @@
         x_copy(k).wait_recv()
         return 0
 
-    lax.fori_loop(0, N_CHAN - 1, send_part, 0)
+    for n in range(N_CHAN - 1):
+        send_part(n, 0)
     parts[pl.ds(0, 32), :] = sums[g]
     for copy in table_copies:
         copy.wait()
@@ -266,11 +277,13 @@
             ).start()
             return 0
 
-        lax.fori_loop(0, N_TM - 1, send, 0)
+        for n in range(N_TM - 1):
+            send(n, 0)
 
     pl.semaphore_wait(ring_sem, 7)
     for half in range(2):
-        lax.fori_loop(max(1, 8 * half), 8 * half + 8, wait_part, 0)
+        for k in range(max(1, 8 * half), 8 * half + 8):
+            wait_part(k, 0)
         send_rows(half)
     samples[chunk(me), :] = parts[pl.ds(me, 16, 32), :]
     all_t = pltpu.make_async_remote_copy(
@@ -320,7 +333,8 @@
         ).start()
         return 0
 
-    lax.fori_loop(0, N_TM - 1, send_band, 0)
+    for n in range(N_TM - 1):
+        send_band(n, 0)
     arrived[me] = outgo[me]
     all_f = pltpu.make_async_remote_copy(
         src_ref=arrived.at[pl.ds(0, N_TM - 1)], dst_ref=arrived.at[pl.ds(0, N_TM - 1)],

time: 50.2 us -> 48.4 us (0.964)
  Pallas kernels: 48.5 us -> 46.8 us
    pallas_call x1, Pallas kernels: 48.5 us -> 46.8 us  [local(): pl.pallas_call(kernel, out_shape=jax.ShapeDtypeStruct((2, 32, 256), F32),...]
where the time goes in v5:
time: 48.4 us; the launch traced here: 48.2 us
  Pallas kernels  46.8 us (97%)
  local copies, waits for them, and re-layouts  1.47 us (3%)
    pallas_call x1, Pallas kernels, local(): pl.pallas_call(kernel, out_shape=jax.ShapeDtypeStruct((2, 32, 256), F32),...  46.8 us
    unnamed x1, local copies, waits for them, and re-layouts  1.47 us

profile of v5, /device:TPU:1, one launch (start us, length us, event | category | flops | bytes accessed | tf_op | source)
XLA Modules:
  0.0 48.2 jit_solution(15718683060459552978)
XLA Ops:
  0.0 46.8 %stack_and_transform.1 = f32[2,32,256]{2,1,0:T(8,128)} custom-call(bf16[256,768]{1,0:T(8,128)(2,1)} %raw.1, s32[2,768]{1,0:T(2,128)} %bitcast.6, s32[2,768]{1,0:T(2,128)} %bitcast.7, s32[2,768]{1,0:T(2,128)} %bitcast.8, bf16[64,128]{1,0:T(8,128)(2,1)} %constant.6.clone.first_in, f32[64,256]{1,0:T(8,128)} %constant.7.clone.twiddle_in, ...), custom_call_target="tpu_custom_call" | custom-call | tf_op jit(solution)/shard_map/stack_and_transform/pallas_call | solution.py:367
  46.8 1.5 %copy.10 = f32[2,256,32]{1,2,0:T(8,128)} copy(f32[2,256,32]{1,2,0:T(8,128)} %bitcast.5) | data formatting | bytes 131072

commit v6 on v5

--- a/solution.py
+++ b/solution.py
@@ -134,9 +134,12 @@
         pl.semaphore_signal(barrier, inc=1, device_id=(me, to_chan(k)), device_id_type=MESH)
         return 0
 
-    lax.fori_loop(1, 8, greet_y, 0)
-    lax.fori_loop(1, 4, greet_z, 0)
-    lax.fori_loop(1, N_CHAN, greet_chan, 0)
+    for d in range(1, 8):
+        greet_y(d, 0)
+    for d in range(1, 4):
+        greet_z(d, 0)
+    for d in range(1, N_CHAN):
+        greet_chan(d, 0)
 
     def chunk(i):
         return pl.ds(pl.multiple_of(i * TC, TC), TC)
@@ -176,7 +179,8 @@
 
     for n in range(N_CHAN - 1):
         send_group(n, 0)
-    lax.fori_loop(1, 8, tell_y, 0)
+    for d in range(1, 8):
+        tell_y(d, 0)
     for copy in table_copies:
         copy.start()
 
@@ -340,6 +344,14 @@
         src_ref=arrived.at[pl.ds(0, N_TM - 1)], dst_ref=arrived.at[pl.ds(0, N_TM - 1)],
         send_sem=send_f, recv_sem=recv_f, device_id=(to_tm(0), g), device_id_type=MESH,
     )
+    def drain(k, _):
+        code_copy(k).wait_send()
+        raw_copy(k).wait_send()
+        x_copy(k).wait_send()
+        return 0
+
+    lax.fori_loop(1, N_CHAN, drain, 0)
+    all_t.wait_send()
     all_f.wait_recv()
     for r in range(2):
         for h in range(2):
@@ -348,14 +360,6 @@
                 [turned[32 * n : 32 * n + 32] for n in range(4)], 1
             )
 
-    def drain(k, _):
-        code_copy(k).wait_send()
-        raw_copy(k).wait_send()
-        x_copy(k).wait_send()
-        return 0
-
-    lax.fori_loop(1, N_CHAN, drain, 0)
-    all_t.wait_send()
     all_f.wait_send()
 
 

time: 48.4 us -> 48.6 us (level); the launches traced: 48.2 us -> 47.7 us
  Pallas kernels: 46.8 us -> 46.2 us
    pallas_call x1, Pallas kernels: 46.8 us -> 46.2 us  [local(): pl.pallas_call(kernel, out_shape=jax.ShapeDtypeStruct((2, 32, 256), F32),...]
where the time goes in v6:
time: 48.6 us; the launch traced here: 47.7 us
  Pallas kernels  46.2 us (95%)
  local copies, waits for them, and re-layouts  1.47 us (3%)
    pallas_call x1, Pallas kernels, local(): pl.pallas_call(kernel, out_shape=jax.ShapeDtypeStruct((2, 32, 256), F32),...  46.2 us
    unnamed x1, local copies, waits for them, and re-layouts  1.47 us

profile of v6, /device:TPU:1, one launch (start us, length us, event | category | flops | bytes accessed | tf_op | source)
XLA Modules:
  0.0 47.7 jit_solution(2106133292907110093)
XLA Ops:
  0.0 46.2 %stack_and_transform.1 = f32[2,32,256]{2,1,0:T(8,128)} custom-call(bf16[256,768]{1,0:T(8,128)(2,1)} %raw.1, s32[2,768]{1,0:T(2,128)} %bitcast.6, s32[2,768]{1,0:T(2,128)} %bitcast.7, s32[2,768]{1,0:T(2,128)} %bitcast.8, bf16[64,128]{1,0:T(8,128)(2,1)} %constant.6.clone.first_in, f32[64,256]{1,0:T(8,128)} %constant.7.clone.twiddle_in, ...), custom_call_target="tpu_custom_call" | custom-call | tf_op jit(solution)/shard_map/stack_and_transform/pallas_call | solution.py:371
  46.2 1.5 %copy.10 = f32[2,256,32]{1,2,0:T(8,128)} copy(f32[2,256,32]{1,2,0:T(8,128)} %bitcast.5) | data formatting | bytes 131072
